TPU v7x, 512 devices: a whole 4x4x16 slice. The times are simulated.
512 devices in a mesh: event: 4 (over x_lo, core), tile: 128 (over y, z, x_hi).
Axes of the slice: x: 4 (x_hi: 2, x_lo: 2; x = x_hi * 2 + x_lo), y: 4, z: 16, core: 2. Of those that a mesh axis runs over, the one named last changes fastest.
Arguments:
- surf_depth: bfloat16 [4, 2048, 4096], P('event', 'tile'), may hold values from 0.019897461 to 0.19921875
- surf_mid: bfloat16 [4, 2048, 4096], P('event', 'tile'), may hold values from 0.019897461 to 0.19921875
- surf_seed: bfloat16 [4, 2048, 4096], P('event', 'tile'), may hold values from -6 to 6
- stream: int32 [2048, 4096], P('tile'), may hold values 0 or 1
- infil: float32 [256, 512], P('tile'), may hold values from 0.05 to 0.4
- diffus: float32 [256, 512], P('tile'), may hold values from 0.03 to 0.12
- leakance: float32 [512, 256], P('tile'), may hold values from 0.005 to 0.05
- active: int32 [512, 256], P('tile'), may hold values 0 or 1
- jacobi_coef: float32 [16, 512, 256], P(None, 'tile'), may hold values from 0.1 to 0.16
- head_seed: float32 [4, 16, 512, 256], P('event', None, 'tile'), may hold values from -6 to 6
- top_head: float32 [4, 512, 256], P('event', 'tile'), may hold values from -0.6 to 0.6
Outputs:
- depth_adj: bfloat16 [4, 2048, 4096], P('event', 'tile')
- head_adj: float32 [4, 16, 512, 256], P('event', None, 'tile')
- recharge_adj: float32 [4, 512, 256], P('event', 'tile')
- grad_w: float32 [256, 512], P('tile')
- grad_g: float32 [256, 512], P('tile')
- grad_lk: float32 [512, 256], P('tile')
All inputs are finite; a program needn't handle non-finite values. No bound on the sum of `stream` or of `active` on one device may be relied on, other than what follows from the above.
Results may differ from a plain program's by a relative error of at most 0.001.
Values sent between devices are 32-bit elements; how exact they have to be, the bound alone decides.
A program may use at most 64 MiB of HBM per device.

v0:
```python
import jax
import jax.numpy as jnp
from jax import lax
from jax.sharding import PartitionSpec as P


def padded(cells, sides, width):
    for axis, dim in sides:
        count = lax.axis_size(axis)
        ends = count - 1
        head = lax.slice_in_dim(cells, 0, width, axis=dim)
        tail = lax.slice_in_dim(cells, cells.shape[dim] - width, cells.shape[dim], axis=dim)
        cells = jnp.concatenate(
            [
                lax.ppermute(tail, axis, [(i, (i + 1) % count) for i in range(ends)]),
                cells,
                lax.ppermute(head, axis, [((i + 1) % count, i) for i in range(ends)]),
            ],
            axis=dim,
        )
    return cells


def laplace_rows(extended):
    center = extended[..., 1:-1, :]
    widened = jnp.pad(center, [(0, 0)] * (center.ndim - 1) + [(1, 1)])
    return (
        extended[..., 2:, :]
        + extended[..., :-2, :]
        + widened[..., 2:]
        + widened[..., :-2]
        - 4.0 * center
    )


def neighbours_cols(extended):
    center = extended[..., 1:-1, :]
    layered = jnp.pad(center, [(0, 0)] * (center.ndim - 3) + [(1, 1), (0, 0), (0, 0)])
    rowwise = jnp.pad(center, [(0, 0)] * (center.ndim - 1) + [(1, 1)])
    return (
        extended[..., 2:, :]
        + extended[..., :-2, :]
        + rowwise[..., 2:]
        + rowwise[..., :-2]
        + layered[..., 2:, :, :]
        + layered[..., :-2, :, :]
    )


def restrict_sum(field):
    shape = field.shape
    blocks = field.reshape(shape[:-2] + (shape[-2] // 8, 8, shape[-1] // 8, 8))
    return jnp.sum(blocks, axis=(-3, -1))


def prolong(coarse):
    shape = coarse.shape
    wide = jnp.broadcast_to(
        coarse[..., :, None, :, None], shape[:-2] + (shape[-2], 8, shape[-1], 8)
    )
    return wide.reshape(shape[:-2] + (shape[-2] * 8, shape[-1] * 8))


def per_device(
    surf_depth,
    surf_mid,
    surf_seed,
    stream,
    infil,
    diffus,
    leakance,
    active,
    jacobi_coef,
    head_seed,
    top_head,
):
    factor = 1.0 + stream.astype(jnp.float32)
    infil_fine = prolong(infil) * factor
    diff_fine = prolong(diffus) * factor
    adj_two = surf_seed.astype(jnp.float32)
    depth = surf_depth.astype(jnp.float32)
    middle = surf_mid.astype(jnp.float32)
    start = depth - infil_fine * depth
    flux_two = diff_fine * adj_two
    start_wide = padded(start, (("tile", 1),), 1)
    middle_wide = padded(middle, (("tile", 1),), 1)
    flux_wide = padded(flux_two, (("tile", 1),), 1)
    adj_one = adj_two + laplace_rows(flux_wide)
    flux_next = padded(diff_fine * adj_one, (("tile", 1),), 1)
    adj_zero = adj_one + laplace_rows(flux_next)
    leak_sum = restrict_sum(factor * (adj_one + adj_two))
    leak_cols = lax.all_to_all(
        jnp.swapaxes(leak_sum, 1, 2), "tile", split_axis=1, concat_axis=2, tiled=True
    )
    head_two = head_seed.at[:, 0].add(leakance * leak_cols)
    coeffs = active.astype(jnp.float32)[None] * jacobi_coef
    weighted = coeffs * head_two
    head_one = neighbours_cols(padded(weighted, (("tile", 2),), 1))
    weighted_next = coeffs * head_one
    head_zero = neighbours_cols(padded(weighted_next, (("tile", 2),), 1))
    charge = weighted[:, 0] + weighted_next[:, 0]
    returned = lax.all_to_all(charge, "tile", split_axis=2, concat_axis=1, tiled=True)
    source_adj = -adj_zero + prolong(jnp.swapaxes(returned, 1, 2))
    depth_adj = (adj_zero + infil_fine * source_adj).astype(jnp.bfloat16)
    local_w = jnp.sum(restrict_sum(factor * depth * source_adj), axis=0)
    local_g = jnp.sum(
        restrict_sum(
            factor * (adj_two * laplace_rows(middle_wide) + adj_one * laplace_rows(start_wide))
        ),
        axis=0,
    )
    local_lk = jnp.sum(top_head * leak_cols, axis=0)
    grad_w, grad_g, grad_lk = lax.psum((local_w, local_g, local_lk), "event")
    return (depth_adj, head_zero, charge, grad_w, grad_g, grad_lk)


def solution(mesh):
    return jax.shard_map(
        per_device,
        mesh=mesh,
        in_specs=(
            P("event", "tile", None),
            P("event", "tile", None),
            P("event", "tile", None),
            P("tile", None),
            P("tile", None),
            P("tile", None),
            P("tile", None),
            P("tile", None),
            P(None, "tile", None),
            P("event", None, "tile", None),
            P("event", "tile", None),
        ),
        out_specs=(
            P("event", "tile", None),
            P("event", None, "tile", None),
            P("event", "tile", None),
            P("tile", None),
            P("tile", None),
            P("tile", None),
        ),
        check_vma=False,
    )
```

profile of v0, /device:TPU:1, one launch (start us, length us, event | category | flops | bytes accessed | tf_op | source)
XLA Modules:
  0.0 168.8 jit_solution(4926096143956133739)
XLA Ops:
  0.6 3.1 %broadcast_in_dim.18 = f32[2,8,512,8]{3,2,1,0:T(8,128)} broadcast(f32[2,512]{1,0:T(2,128)} %param.18), dimensions={0,2} | broadcast | bytes 266240 | tf_op jit(solution)/shard_map/broadcast_in_dim | solution.py:58
  3.7 4.0 %reshape.108 = f32[16,4096]{1,0:T(8,128)S(1)} reshape(f32[2,8,512,8]{3,2,1,0:T(8,128)} %broadcast_in_dim.18) | data formatting | bytes 524288 | tf_op jit(solution)/shard_map/reshape | solution.py:61
  7.7 0.0 copy-start
  7.7 0.0 copy-start.1
  7.8 0.0 copy-start.2
  7.8 0.0 copy-start.4
  7.8 2.4 %broadcast_in_dim.20 = f32[2,8,512,8]{3,2,1,0:T(8,128)} broadcast(f32[2,512]{1,0:T(2,128)S(1)} %copy-done.6), dimensions={0,2} | broadcast | bytes 266240 | tf_op jit(solution)/shard_map/broadcast_in_dim | solution.py:58
  10.2 4.0 %reshape.109 = f32[16,4096]{1,0:T(8,128)S(1)} reshape(f32[2,8,512,8]{3,2,1,0:T(8,128)} %broadcast_in_dim.20) | data formatting | bytes 524288 | tf_op jit(solution)/shard_map/reshape | solution.py:61
  14.2 0.1 convert_multiply_fusion.1
  14.4 1.3 collective-permute-start
  15.7 6.1 %collective-permute-start.1 = (f32[1,1,4096]{2,1,0:T(1,128)S(1)}, f32[1,1,4096]{2,1,0:T(1,128)S(1)}, u32[]{:S(2)}, u32[]{:S(2)}) collective-permute-start(f32[1,1,4096]{2,1,0:T(1,128)S(1)} %get-tuple-element.54), channel_id=1, source_target_pairs={{0,1},{1,2},{2,3},{3,4},{4,5},{5,6},{6,7},{7,8},{8,9},{9,10},{10,1... | collective-permute-start | bytes 49160 | tf_op jit(solution)/shard_map/ppermute | solution.py:15
  21.8 1.3 collective-permute-start.10
  23.1 6.4 %collective-permute-start.11 = (f32[1,1,4096]{2,1,0:T(1,128)S(1)}, f32[1,1,4096]{2,1,0:T(1,128)S(1)}, u32[]{:S(2)}, u32[]{:S(2)}) collective-permute-start(f32[1,1,4096]{2,1,0:T(1,128)S(1)} %get-tuple-element.58), channel_id=1, source_target_pairs={{0,1},{1,2},{2,3},{3,4},{4,5},{5,6},{6,7},{7,8},{8,9},{9,10},{10,1... | collective-permute-start | bytes 49160 | tf_op jit(solution)/shard_map/ppermute | solution.py:15
  29.6 1.3 collective-permute-start.8
  30.9 0.0 collective-permute-done
  30.9 6.4 %collective-permute-start.9 = (f32[1,1,4096]{2,1,0:T(1,128)S(1)}, f32[1,1,4096]{2,1,0:T(1,128)S(1)}, u32[]{:S(2)}, u32[]{:S(2)}) collective-permute-start(f32[1,1,4096]{2,1,0:T(1,128)S(1)} %get-tuple-element.60), channel_id=1, source_target_pairs={{0,1},{1,2},{2,3},{3,4},{4,5},{5,6},{6,7},{7,8},{8,9},{9,10},{10,1... | collective-permute-start | bytes 49160 | tf_op jit(solution)/shard_map/ppermute | solution.py:15
  37.4 0.1 copy.64
  37.5 0.0 collective-permute-done.1
  37.5 0.0 collective-permute-done.10
  37.5 0.0 collective-permute-done.11
  37.5 0.0 collective-permute-done.8
  37.5 0.6 collective-permute-done.9
  38.1 0.6 fusion.3
  38.8 0.1 bitcast_multiply_fusion.1
  38.8 3.6 %reshape.110 = f32[2,8,512,8]{3,2,1,0:T(8,128)} reshape(f32[1,16,4096]{2,1,0:T(8,128)S(1)} %get-tuple-element.50) | data formatting | bytes 524288 | tf_op jit(solution)/shard_map/reshape | solution.py:52
  42.5 2.5 %reduce_sum.34 = f32[2,512]{1,0:T(2,128)S(1)} reduce(f32[2,8,512,8]{3,2,1,0:T(8,128)} %reshape.110, f32[]{:T(128)} %constant.32.clone.1), dimensions={1,3}, to_apply=%region_0.1 | reduce | flops 64512 | bytes 266244 | tf_op jit(solution)/shard_map/reduce_sum | solution.py:53
  45.0 0.9 copy.55
  45.9 27.0 %all-to-all-start = ((f32[1,512,2]{2,0,1:T(1,128)}), f32[1,512,2]{2,0,1:T(1,128)S(1)}, u32[]{:S(2)}, u32[]{:S(2)}) async-start(f32[1,512,2]{2,0,1:T(1,128)} %copy.55), calls=%async_computation | async-start | bytes 524288 | tf_op jit(solution)/shard_map/all_to_all | solution.py:92
  72.9 1.3 collective-permute-start.2
  74.2 5.5 %collective-permute-start.3 = (f32[1,1,4096]{2,1,0:T(1,128)S(1)}, f32[1,1,4096]{2,1,0:T(1,128)S(1)}, u32[]{:S(2)}, u32[]{:S(2)}) collective-permute-start(f32[1,1,4096]{2,1,0:T(1,128)S(1)} %get-tuple-element.52), channel_id=1, source_target_pairs={{0,1},{1,2},{2,3},{3,4},{4,5},{5,6},{6,7},{7,8},{8,9},{9,10},{10,1... | collective-permute-start | bytes 49160 | tf_op jit(solution)/shard_map/ppermute | solution.py:15
  79.7 0.0 copy-start.9
  79.7 0.0 copy-start.3
  79.7 3.6 %reshape.113 = f32[2,8,512,8]{3,2,1,0:T(8,128)} reshape(f32[1,16,4096]{2,1,0:T(8,128)S(1)} %get-tuple-element.45) | data formatting | bytes 524288 | tf_op jit(solution)/shard_map/reshape | solution.py:52
  83.3 2.5 %reduce_sum.37 = f32[2,512]{1,0:T(2,128)S(1)} reduce(f32[2,8,512,8]{3,2,1,0:T(8,128)} %reshape.113, f32[]{:T(128)} %constant.32.clone.1), dimensions={1,3}, to_apply=%region_3.4 | reduce | flops 64512 | bytes 266244 | tf_op jit(solution)/shard_map/reduce_sum | solution.py:53
  85.9 6.6 %all-to-all-done = f32[1,512,2]{2,0,1:T(1,128)S(1)} async-done(((f32[1,512,2]{2,0,1:T(1,128)}), f32[1,512,2]{2,0,1:T(1,128)S(1)}, u32[]{:S(2)}, u32[]{:S(2)}) %all-to-all-start) | async-done | bytes 4128 | tf_op jit(solution)/shard_map/all_to_all | solution.py:92
  92.4 0.9 copy.68
  93.4 0.1 copy.57
  93.5 0.1 copy.58
  93.7 1.3 collective-permute-start.4
  95.0 5.5 %collective-permute-start.5 = (f32[1,16,1,256]{3,1,2,0:T(8,128)S(1)}, f32[1,16,1,256]{3,1,2,0:T(8,128)S(1)}, u32[]{:S(2)}, u32[]{:S(2)}) collective-permute-start(f32[1,16,1,256]{3,1,2,0:T(8,128)S(1)} %get-tuple-element.64), channel_id=1, source_target_pairs={{0,1},{1,2},{2,3},{3,4},{4,5},{5,6},{6,7},{7,8},{8,9},{9,10},{10,1... | collective-permute-start | bytes 49160 | tf_op jit(solution)/shard_map/ppermute | solution.py:15
  100.5 0.0 collective-permute-done.4
  100.5 0.8 collective-permute-done.5
  101.3 0.1 fusion.30
  101.5 0.8 copy.61
  102.3 16.2 %all-to-all-start.1 = ((f32[1,4,256]{1,0,2:T(1,128)}), f32[1,4,256]{1,0,2:T(1,128)S(1)}, u32[]{:S(2)}, u32[]{:S(2)}) async-start(f32[1,4,256]{1,0,2:T(1,128)} %copy.61), calls=%async_computation.1 | async-start | bytes 262144 | tf_op jit(solution)/shard_map/all_to_all | solution.py:102
  118.5 0.6 copy.66
  119.1 1.3 collective-permute-start.6
  120.4 5.7 %collective-permute-start.7 = (f32[1,16,1,256]{3,1,2,0:T(8,128)S(1)}, f32[1,16,1,256]{3,1,2,0:T(8,128)S(1)}, u32[]{:S(2)}, u32[]{:S(2)}) collective-permute-start(f32[1,16,1,256]{3,1,2,0:T(8,128)S(1)} %get-tuple-element.62), channel_id=1, source_target_pairs={{0,1},{1,2},{2,3},{3,4},{4,5},{5,6},{6,7},{7,8},{8,9},{9,10},{10,1... | collective-permute-start | bytes 49160 | tf_op jit(solution)/shard_map/ppermute | solution.py:15
  126.1 9.3 %all-to-all-done.1 = f32[1,4,256]{1,0,2:T(1,128)S(1)} async-done(((f32[1,4,256]{1,0,2:T(1,128)}), f32[1,4,256]{1,0,2:T(1,128)S(1)}, u32[]{:S(2)}, u32[]{:S(2)}) %all-to-all-start.1) | async-done | bytes 4128 | tf_op jit(solution)/shard_map/all_to_all | solution.py:102
  135.4 0.1 all_to_all.35
  135.5 2.4 %broadcast_in_dim.48 = f32[2,8,512,8]{3,2,1,0:T(8,128)} broadcast(f32[2,512]{1,0:T(2,128)S(1)} %bitcast.52), dimensions={0,2} | broadcast | bytes 266240 | tf_op jit(solution)/shard_map/broadcast_in_dim | solution.py:58
  137.9 4.0 %broadcast_in_dim.49 = f32[1,16,4096]{2,1,0:T(8,128)S(1)} reshape(f32[2,8,512,8]{3,2,1,0:T(8,128)} %broadcast_in_dim.48) | data formatting | bytes 524288 | tf_op jit(solution)/shard_map/broadcast_in_dim | solution.py:58
  141.9 0.0 collective-permute-done.2
  141.9 0.0 collective-permute-done.3
  141.9 0.2 fusion
  142.2 0.7 fusion.23
  142.9 3.6 %reshape.112 = f32[2,8,512,8]{3,2,1,0:T(8,128)} reshape(f32[1,16,4096]{2,1,0:T(8,128)S(1)} %get-tuple-element.47) | data formatting | bytes 524288 | tf_op jit(solution)/shard_map/reshape | solution.py:52
  146.5 2.5 %reduce_sum.36 = f32[2,512]{1,0:T(2,128)S(1)} reduce(f32[2,8,512,8]{3,2,1,0:T(8,128)} %reshape.112, f32[]{:T(128)} %constant.32.clone.1), dimensions={1,3}, to_apply=%region_1.2 | reduce | flops 64512 | bytes 266244 | tf_op jit(solution)/shard_map/reduce_sum | solution.py:53
  149.0 18.3 %all-reduce.8 = (f32[2,512]{1,0:T(2,128)}, f32[2,512]{1,0:T(2,128)}, f32[4,256]{0,1:T(8,128)S(1)}) all-reduce(f32[2,512]{1,0:T(2,128)S(1)} %reduce_sum.36, f32[2,512]{1,0:T(2,128)S(1)} %reduce_sum.37, f32[4,256]{0,1:T(8,128)S(1)} %multiply_bitcast_fusion), channel_id=1, replica_groups=mesh['event'=4,'tile'=128] {'event'}, use_global_device_ids=true, to_apply=%region_2.3 | all-reduce | flops 3072 | bytes 24576 | tf_op jit(solution)/shard_map/psum | solution.py:113
  167.3 0.7 copy.67
  168.0 0.0 collective-permute-done.6
  168.0 0.0 collective-permute-done.7
  168.0 0.1 fusion.34
  168.1 0.7 copy.65
  (30 shorter events, 0.3 us)
Async XLA Ops:
  0.6 7.1 %copy-start.6 = (f32[2,512]{1,0:T(2,128)S(1)}, f32[2,512]{1,0:T(2,128)}, u32[]{:S(2)}) copy-start(f32[2,512]{1,0:T(2,128)} %param.17) | copy-start | bytes 12292
  7.7 6.5 %copy-start = (s32[16,4096]{1,0:T(8,128)S(1)}, s32[16,4096]{1,0:T(8,128)}, u32[]{:S(2)}) copy-start(s32[16,4096]{1,0:T(8,128)} %param.16) | copy-start | bytes 786436
  7.7 6.5 %copy-start.1 = (bf16[1,16,4096]{2,1,0:T(8,128)(2,1)S(1)}, bf16[1,16,4096]{2,1,0:T(8,128)(2,1)}, u32[]{:S(2)}) copy-start(bf16[1,16,4096]{2,1,0:T(8,128)(2,1)} %param.15) | copy-start | bytes 393220
  7.8 6.5 %copy-start.2 = (bf16[1,16,4096]{2,1,0:T(8,128)(2,1)S(1)}, bf16[1,16,4096]{2,1,0:T(8,128)(2,1)}, u32[]{:S(2)}) copy-start(bf16[1,16,4096]{2,1,0:T(8,128)(2,1)} %param.13) | copy-start | bytes 393220
  7.8 21.7 %copy-start.4 = (bf16[1,16,4096]{2,1,0:T(8,128)(2,1)S(1)}, bf16[1,16,4096]{2,1,0:T(8,128)(2,1)}, u32[]{:S(2)}) copy-start(bf16[1,16,4096]{2,1,0:T(8,128)(2,1)} %param.14) | copy-start | bytes 393220
  10.2 27.1 %copy-start.5 = (f32[1,16,4,256]{3,2,1,0:T(4,128)S(1)}, f32[1,16,4,256]{3,2,1,0:T(4,128)}, u32[]{:S(2)}) copy-start(f32[1,16,4,256]{3,2,1,0:T(4,128)} %param.22) | copy-start | bytes 196612
  10.2 27.1 %copy-start.8 = (s32[4,256]{1,0:T(4,128)S(1)}, s32[4,256]{1,0:T(4,128)}, u32[]{:S(2)}) copy-start(s32[4,256]{1,0:T(4,128)} %param.20) | copy-start | bytes 12292
  10.2 27.2 %copy-start.7 = (f32[1,4,256]{2,1,0:T(4,128)S(1)}, f32[1,4,256]{2,1,0:T(4,128)}, u32[]{:S(2)}) copy-start(f32[1,4,256]{2,1,0:T(4,128)} %param.23) | copy-start | bytes 12292
  14.4 16.5 %collective-permute-start = (f32[1,1,4096]{2,1,0:T(1,128)S(1)}, f32[1,1,4096]{2,1,0:T(1,128)S(1)}, u32[]{:S(2)}, u32[]{:S(2)}) collective-permute-start(f32[1,1,4096]{2,1,0:T(1,128)S(1)} %get-tuple-element.53), channel_id=1, source_target_pairs={{1,0},{2,1},{3,2},{4,3},{5,4},{6,5},{7,6},{8,7},{9,8},{10,9},{11,1... | collective-permute-start | bytes 49160 | tf_op jit(solution)/shard_map/ppermute | solution.py:17
  15.7 21.8 %collective-permute-start.1 = (f32[1,1,4096]{2,1,0:T(1,128)S(1)}, f32[1,1,4096]{2,1,0:T(1,128)S(1)}, u32[]{:S(2)}, u32[]{:S(2)}) collective-permute-start(f32[1,1,4096]{2,1,0:T(1,128)S(1)} %get-tuple-element.54), channel_id=1, source_target_pairs={{0,1},{1,2},{2,3},{3,4},{4,5},{5,6},{6,7},{7,8},{8,9},{9,10},{10,1... | collective-permute-start | bytes 49160 | tf_op jit(solution)/shard_map/ppermute | solution.py:15
  21.8 15.7 %collective-permute-start.10 = (f32[1,1,4096]{2,1,0:T(1,128)S(1)}, f32[1,1,4096]{2,1,0:T(1,128)S(1)}, u32[]{:S(2)}, u32[]{:S(2)}) collective-permute-start(f32[1,1,4096]{2,1,0:T(1,128)S(1)} %get-tuple-element.57), channel_id=1, source_target_pairs={{1,0},{2,1},{3,2},{4,3},{5,4},{6,5},{7,6},{8,7},{9,8},{10,9},{11,1... | collective-permute-start | bytes 49160 | tf_op jit(solution)/shard_map/ppermute | solution.py:17
  23.1 14.4 %collective-permute-start.11 = (f32[1,1,4096]{2,1,0:T(1,128)S(1)}, f32[1,1,4096]{2,1,0:T(1,128)S(1)}, u32[]{:S(2)}, u32[]{:S(2)}) collective-permute-start(f32[1,1,4096]{2,1,0:T(1,128)S(1)} %get-tuple-element.58), channel_id=1, source_target_pairs={{0,1},{1,2},{2,3},{3,4},{4,5},{5,6},{6,7},{7,8},{8,9},{9,10},{10,1... | collective-permute-start | bytes 49160 | tf_op jit(solution)/shard_map/ppermute | solution.py:15
  29.6 8.0 %collective-permute-start.8 = (f32[1,1,4096]{2,1,0:T(1,128)S(1)}, f32[1,1,4096]{2,1,0:T(1,128)S(1)}, u32[]{:S(2)}, u32[]{:S(2)}) collective-permute-start(f32[1,1,4096]{2,1,0:T(1,128)S(1)} %get-tuple-element.59), channel_id=1, source_target_pairs={{1,0},{2,1},{3,2},{4,3},{5,4},{6,5},{7,6},{8,7},{9,8},{10,9},{11,1... | collective-permute-start | bytes 49160 | tf_op jit(solution)/shard_map/ppermute | solution.py:17
  30.9 7.3 %collective-permute-start.9 = (f32[1,1,4096]{2,1,0:T(1,128)S(1)}, f32[1,1,4096]{2,1,0:T(1,128)S(1)}, u32[]{:S(2)}, u32[]{:S(2)}) collective-permute-start(f32[1,1,4096]{2,1,0:T(1,128)S(1)} %get-tuple-element.60), channel_id=1, source_target_pairs={{0,1},{1,2},{2,3},{3,4},{4,5},{5,6},{6,7},{7,8},{8,9},{9,10},{10,1... | collective-permute-start | bytes 49160 | tf_op jit(solution)/shard_map/ppermute | solution.py:15
  45.9 46.6 %all-to-all-start = ((f32[1,512,2]{2,0,1:T(1,128)}), f32[1,512,2]{2,0,1:T(1,128)S(1)}, u32[]{:S(2)}, u32[]{:S(2)}) async-start(f32[1,512,2]{2,0,1:T(1,128)} %copy.55), calls=%async_computation | async-start | bytes 524288 | tf_op jit(solution)/shard_map/all_to_all | solution.py:92
  72.9 69.0 %collective-permute-start.2 = (f32[1,1,4096]{2,1,0:T(1,128)S(1)}, f32[1,1,4096]{2,1,0:T(1,128)S(1)}, u32[]{:S(2)}, u32[]{:S(2)}) collective-permute-start(f32[1,1,4096]{2,1,0:T(1,128)S(1)} %get-tuple-element.51), channel_id=1, source_target_pairs={{1,0},{2,1},{3,2},{4,3},{5,4},{6,5},{7,6},{8,7},{9,8},{10,9},{11,1... | collective-permute-start | bytes 49160 | tf_op jit(solution)/shard_map/ppermute | solution.py:17
  74.2 67.7 %collective-permute-start.3 = (f32[1,1,4096]{2,1,0:T(1,128)S(1)}, f32[1,1,4096]{2,1,0:T(1,128)S(1)}, u32[]{:S(2)}, u32[]{:S(2)}) collective-permute-start(f32[1,1,4096]{2,1,0:T(1,128)S(1)} %get-tuple-element.52), channel_id=1, source_target_pairs={{0,1},{1,2},{2,3},{3,4},{4,5},{5,6},{6,7},{7,8},{8,9},{9,10},{10,1... | collective-permute-start | bytes 49160 | tf_op jit(solution)/shard_map/ppermute | solution.py:15
  79.7 13.9 %copy-start.9 = (f32[4,256]{1,0:T(4,128)S(1)}, f32[4,256]{1,0:T(4,128)}, u32[]{:S(2)}) copy-start(f32[4,256]{1,0:T(4,128)} %param.19) | copy-start | bytes 12292
  79.7 14.0 %copy-start.3 = (f32[16,4,256]{2,1,0:T(4,128)S(1)}, f32[16,4,256]{2,1,0:T(4,128)}, u32[]{:S(2)}) copy-start(f32[16,4,256]{2,1,0:T(4,128)} %param.21) | copy-start | bytes 196612
  93.7 6.8 %collective-permute-start.4 = (f32[1,16,1,256]{3,1,2,0:T(8,128)S(1)}, f32[1,16,1,256]{3,1,2,0:T(8,128)S(1)}, u32[]{:S(2)}, u32[]{:S(2)}) collective-permute-start(f32[1,16,1,256]{3,1,2,0:T(8,128)S(1)} %get-tuple-element.63), channel_id=1, source_target_pairs={{1,0},{2,1},{3,2},{4,3},{5,4},{6,5},{7,6},{8,7},{9,8},{10,9},{11,1... | collective-permute-start | bytes 49160 | tf_op jit(solution)/shard_map/ppermute | solution.py:17
  95.0 6.4 %collective-permute-start.5 = (f32[1,16,1,256]{3,1,2,0:T(8,128)S(1)}, f32[1,16,1,256]{3,1,2,0:T(8,128)S(1)}, u32[]{:S(2)}, u32[]{:S(2)}) collective-permute-start(f32[1,16,1,256]{3,1,2,0:T(8,128)S(1)} %get-tuple-element.64), channel_id=1, source_target_pairs={{0,1},{1,2},{2,3},{3,4},{4,5},{5,6},{6,7},{7,8},{8,9},{9,10},{10,1... | collective-permute-start | bytes 49160 | tf_op jit(solution)/shard_map/ppermute | solution.py:15
  102.3 33.1 %all-to-all-start.1 = ((f32[1,4,256]{1,0,2:T(1,128)}), f32[1,4,256]{1,0,2:T(1,128)S(1)}, u32[]{:S(2)}, u32[]{:S(2)}) async-start(f32[1,4,256]{1,0,2:T(1,128)} %copy.61), calls=%async_computation.1 | async-start | bytes 262144 | tf_op jit(solution)/shard_map/all_to_all | solution.py:102
  119.1 48.9 %collective-permute-start.6 = (f32[1,16,1,256]{3,1,2,0:T(8,128)S(1)}, f32[1,16,1,256]{3,1,2,0:T(8,128)S(1)}, u32[]{:S(2)}, u32[]{:S(2)}) collective-permute-start(f32[1,16,1,256]{3,1,2,0:T(8,128)S(1)} %get-tuple-element.61), channel_id=1, source_target_pairs={{1,0},{2,1},{3,2},{4,3},{5,4},{6,5},{7,6},{8,7},{9,8},{10,9},{11,1... | collective-permute-start | bytes 49160 | tf_op jit(solution)/shard_map/ppermute | solution.py:17
  120.4 47.6 %collective-permute-start.7 = (f32[1,16,1,256]{3,1,2,0:T(8,128)S(1)}, f32[1,16,1,256]{3,1,2,0:T(8,128)S(1)}, u32[]{:S(2)}, u32[]{:S(2)}) collective-permute-start(f32[1,16,1,256]{3,1,2,0:T(8,128)S(1)} %get-tuple-element.62), channel_id=1, source_target_pairs={{0,1},{1,2},{2,3},{3,4},{4,5},{5,6},{6,7},{7,8},{8,9},{9,10},{10,1... | collective-permute-start | bytes 49160 | tf_op jit(solution)/shard_map/ppermute | solution.py:15
where the time goes:
time: 169 us
  starting transfers between devices  86.5 us (51%)
  local copies, waits for them, and re-layouts  36 us (21%)
  blocking collectives  18.3 us (11%)
  waiting for transfers between devices  17.3 us (10%)
  other arithmetic  9.66 us (6%)
    ppermute x6, starting transfers between devices, padded(): lax.ppermute(tail, axis, [(i, (i + 1) % count) for i in range(ends)])  35.5 us
    all_to_all x1, starting transfers between devices, per_device(): lax.all_to_all(jnp.swapaxes(leak_sum, 1, 2), 'tile', split_axis=1, concat...  27 us
    psum x1, blocking collectives, per_device(): grad_w, grad_g, grad_lk = lax.psum((local_w, local_g, local_lk), 'event')  18.3 us
    all_to_all x1, starting transfers between devices, per_device(): lax.all_to_all(charge, 'tile', split_axis=2, concat_axis=1, tiled=True)  16.2 us
    broadcast_in_dim x4, local copies, waits for them, and re-layouts, prolong(): jnp.broadcast_to(coarse[..., :, None, :, None], shape[:-2] + (shape[-2],...  11.9 us
    reshape x3, local copies, waits for them, and re-layouts, restrict_sum(): blocks = field.reshape(shape[:-2] + (shape[-2] // 8, 8, shape[-1] // 8, 8))  10.8 us
    all_to_all x1, waiting for transfers between devices, per_device(): lax.all_to_all(charge, 'tile', split_axis=2, concat_axis=1, tiled=True)  9.29 us
    reshape x2, local copies, waits for them, and re-layouts, prolong(): return wide.reshape(shape[:-2] + (shape[-2] * 8, shape[-1] * 8))  7.98 us
  transfers between devices with their start and end apart: 14, of which 4 were waited for; matrix products, arithmetic and copies ran while one was open for 14% of the time, Pallas kernels for 0%

commit v1 on v0

v1 whole, which is shorter than its diff:
```python
import functools

import jax
import jax.numpy as jnp
from jax import lax
from jax.experimental import pallas as pl
from jax.experimental.pallas import tpu as pltpu
from jax.sharding import PartitionSpec as P

MESH = pl.DeviceIdType.MESH
F32 = jnp.float32
BF16 = jnp.bfloat16
TILES, EVENTS = 128, 4
ROWS, COLS = 16, 4096
LAYERS, OWN, AROWS, ACOLS = 16, 4, 256, 512
NEAR = (0, 1, 15, 8, 7, 9, 6, 10, 5, 11, 4, 12, 3, 13, 2, 14)
FAR = (8, 7, 9, 6, 10, 5, 11, 4, 12, 3, 13, 2, 14, 1, 15, 0)
PLANE = ((2, 1), (2, 0), (1, 1), (3, 1), (1, 0), (3, 0), (0, 1), (0, 0))


def iota(shape, dim):
    return lax.broadcasted_iota(jnp.int32, shape, dim)


def lanes_by(field, shift):
    n = field.shape[-1]
    lane = iota(field.shape, field.ndim - 1)
    inside = lane >= shift if shift > 0 else lane < n + shift
    return jnp.where(inside, pltpu.roll(field, shift % n, axis=field.ndim - 1), 0.0)


def laplace_inner(field):
    row = iota(field.shape, 0)
    above = jnp.where(row == 0, 0.0, pltpu.roll(field, 1, axis=0))
    below = jnp.where(row == ROWS - 1, 0.0, pltpu.roll(field, ROWS - 1, axis=0))
    return below + above + lanes_by(field, -1) + lanes_by(field, 1) - 4.0 * field


def edges(top, bottom):
    row = iota((ROWS, top.shape[-1]), 0)
    return jnp.where(row == 0, top, 0.0) + jnp.where(row == ROWS - 1, bottom, 0.0)


def pieces(values, axis):
    high = values.astype(BF16).astype(F32)
    return jnp.concatenate([high, values - high], axis=axis).astype(BF16)


def compress(field, block_ref):
    n = field.shape[0]
    wide = jnp.concatenate([field[:, q * 1024 : (q + 1) * 1024] for q in range(4)], axis=0)
    out = jnp.dot(pieces(wide, 0), block_ref[...], preferred_element_type=F32)
    out = out[: 4 * n] + out[4 * n :]
    return jnp.concatenate([out[q * n : (q + 1) * n] for q in range(4)], axis=1)


def block_sums(field, block_ref):
    part = compress(field, block_ref)
    return jnp.concatenate(
        [jnp.sum(part[:8], axis=0, keepdims=True), jnp.sum(part[8:], axis=0, keepdims=True)], axis=0
    )


def prolong(coarse):
    halves = []
    spot = iota((8, 128), 1) // 8
    for r in range(2):
        parts = []
        for m in range(COLS // 128):
            q, s = divmod(m, 8)
            source = jnp.broadcast_to(coarse[r : r + 1, q * 128 : (q + 1) * 128], (8, 128))
            parts.append(
                jnp.take_along_axis(source, spot + 16 * s, axis=1, mode="promise_in_bounds")
            )
        halves.append(jnp.concatenate(parts, axis=1))
    return jnp.concatenate(halves, axis=0)


def pad_rows(rows, n):
    return jnp.concatenate([rows, jnp.zeros((n - rows.shape[0], rows.shape[1]), F32)], axis=0)


def neighbours4(field):
    dim = field.ndim - 2
    return (
        pltpu.roll(field, 7, axis=dim)
        + pltpu.roll(field, 1, axis=dim)
        + lanes_by(field, -1)
        + lanes_by(field, 1)
    )


def step_kernel(
    seed_h, stream_h, diffus_h, jac_h, act_h, leak_h, head_h, infil_h, depth_h, mid_h, top_h,
    depth_o, head_o, charge_o, gw_o, gg_o, glk_o,
    seed_v, stream_v, diffus_v, jac_v, act_v, leak_v, head_v, infil_v, depth_v, mid_v, top_v,
    factor, diff, fluxes, adj1, scaled, startv, block_w,
    fs, fr, hs, hr, ls, lr, cw, xs, ms, mr, ns, nr, ev1, ev2,
    in_sem, edge_send, edge_recv, a2a_send, a2a_recv, ev_send, ev_recv,
):
    e = lax.axis_index("event")
    t = lax.axis_index("tile")
    y, z, x = t // 32, (t // 2) % 16, t % 2
    below, above = (t + 1) % TILES, (t + TILES - 1) % TILES
    has_below, has_above = t < TILES - 1, t > 0

    def each_tile(order, act):
        def body(i, carry):
            h = (i + 1) // 2
            dz = order(i, h)
            for dy, dx in PLANE:
                act((((y + dy) % 4) * 16 + (z + dz) % 16) * 2 + (x + dx) % 2)
            return carry

        lax.fori_loop(0, 15, body, 0)
        for dy, dx in PLANE:
            if dy or dx:
                act((((y + dy) % 4) * 16 + z) * 2 + (x + dx) % 2)

    def far_first(i, h):
        return jnp.where(i % 2 == 1, 8 - h, 8 + h)

    loads = [
        pltpu.make_async_copy(src, dst, in_sem.at[n])
        for n, (src, dst) in enumerate(
            zip(
                (seed_h, stream_h, diffus_h, jac_h, act_h, leak_h, head_h, infil_h, depth_h, mid_h, top_h),
                (seed_v, stream_v, diffus_v, jac_v, act_v, leak_v, head_v, infil_v, depth_v, mid_v, top_v),
            )
        )
    ]
    for load in loads:
        load.start()

    barrier = pltpu.get_barrier_semaphore()
    for k in range(1, EVENTS):
        pl.semaphore_signal(barrier, inc=1, device_id=((e + k) % EVENTS, t), device_id_type=MESH)
    each_tile(
        far_first,
        lambda d: pl.semaphore_signal(barrier, inc=1, device_id=(e, d), device_id_type=MESH),
    )

    for load in loads:
        load.wait()

    block_w[...] = (iota((1024, 128), 0) // 8 == iota((1024, 128), 1)).astype(F32).astype(BF16)
    ns[...] = jnp.zeros((TILES, 128), F32)
    ms[...] = jnp.zeros((TILES, 128), F32)
    factor[...] = 1.0 + stream_v[...].astype(F32)
    diff[...] = prolong(diffus_v[...]) * factor[...]
    seed = seed_v[...].astype(F32)
    fluxes[...] = diff[...] * seed
    fs[0] = fluxes[0:1, :]
    fs[1] = fluxes[ROWS - 1 : ROWS, :]
    adj1[...] = seed + laplace_inner(fluxes[...])
    leak_part = block_sums(factor[...] * (adj1[...] + seed), block_w)
    scaled[...] = diff[...] * adj1[...]
    infil_fine = prolong(infil_v[...]) * factor[...]
    depth = depth_v[...].astype(F32)
    startv[...] = depth - infil_fine * depth
    middle = mid_v[...].astype(F32)
    for way, at in ((0, 0), (1, ROWS - 1)):
        hs[way, 0:1, :] = factor[at : at + 1, :]
        hs[way, 1:2, :] = scaled[at : at + 1, :]
        hs[way, 2:3, :] = diff[at : at + 1, :]
        hs[way, 3:4, :] = startv[at : at + 1, :]
        hs[way, 4:5, :] = middle[at : at + 1, :]
        ls[way] = leak_part[way : way + 1]

    coeffs = act_v[...].astype(F32)[None] * jac_v[...]
    weighted = coeffs * head_v[...]
    leak_coef = coeffs[0] * leak_v[...]
    cw[0:LAYERS, 0:OWN, :] = coeffs
    cw[LAYERS : 2 * LAYERS, 0:OWN, :] = weighted
    cw[2 * LAYERS, 0:OWN, :] = leak_coef
    for k, part in enumerate((weighted[0], leak_coef, coeffs[0], weighted[1])):
        for r in range(4):
            moved = part if r == 1 else lanes_by(part, 1 - r)
            xs[pl.ds(k * 4 + r, 4, stride=16), :] = moved[:, :128]
            xs[pl.ds(64 + k * 4 + r, 4, stride=16), :] = moved[:, 128:]
    pick = (iota((TILES, AROWS), 1) == 2 * iota((TILES, AROWS), 0)).astype(F32).astype(BF16)
    ms[:, 0:64] = lax.dot_general(
        jnp.concatenate([pick, pick], axis=1),
        pieces(jnp.concatenate([xs[0:64, :], xs[64:128, :]], axis=1), 1),
        (((1,), (1,)), ((), ())),
        preferred_element_type=F32,
    )

    pl.semaphore_wait(barrier, TILES - 1 + EVENTS - 1)

    def edge_copy(n, src, dst, target):
        return pltpu.make_async_remote_copy(
            src_ref=src,
            dst_ref=dst,
            send_sem=edge_send.at[n],
            recv_sem=edge_recv.at[n],
            device_id=(e, target),
            device_id_type=MESH,
        )

    flux_copies = [edge_copy(0, fs.at[0], fr.at[0], above), edge_copy(1, fs.at[1], fr.at[1], below)]
    leak_copies = [edge_copy(2, ls.at[0], lr.at[0], above), edge_copy(3, ls.at[1], lr.at[1], below)]
    bulk_copies = [edge_copy(4, hs.at[0], hr.at[0], above), edge_copy(5, hs.at[1], hr.at[1], below)]
    head_copies = [
        edge_copy(6, cw.at[:, pl.ds(0, 2), :], cw.at[:, pl.ds(4, 2), :], above),
        edge_copy(7, cw.at[:, pl.ds(2, 2), :], cw.at[:, pl.ds(6, 2), :], below),
    ]
    for copy in flux_copies + leak_copies + bulk_copies:
        copy.start()

    def to_owner(n, src, dst):
        def act(d):
            pltpu.make_async_remote_copy(
                src_ref=src.at[pl.ds(d, 1)],
                dst_ref=dst.at[pl.ds(t, 1)],
                send_sem=a2a_send.at[n],
                recv_sem=a2a_recv.at[n],
                device_id=(e, d),
                device_id_type=MESH,
            ).start()

        return act

    def all_of(n, src, dst):
        return pltpu.make_async_remote_copy(
            src_ref=src.at[pl.ds(0, TILES - 1)],
            dst_ref=dst.at[pl.ds(0, TILES - 1)],
            send_sem=a2a_send.at[n],
            recv_sem=a2a_recv.at[n],
            device_id=(e, below),
            device_id_type=MESH,
        )

    mr[pl.ds(t, 1), :] = ms[pl.ds(t, 1), :]
    each_tile(far_first, to_owner(0, ms, mr))
    for copy in head_copies:
        copy.start()

    for copy in flux_copies:
        copy.wait()
    flux_below = jnp.where(has_below, fr[0], 0.0)
    flux_above = jnp.where(has_above, fr[1], 0.0)
    own_edges = compress(
        pad_rows(
            jnp.concatenate(
                [factor[0:1, :] * flux_above, factor[ROWS - 1 : ROWS, :] * flux_below], axis=0
            ),
            8,
        ),
        block_w,
    )
    leak_own = leak_part + own_edges[0:2]
    wide = jnp.concatenate(
        [lanes_by(leak_own, -c) if c else leak_own for c in (0, 1, 2, 3, 4, 5, -2, -1)], axis=0
    )
    every = (iota((TILES, ACOLS), 1) == 4 * iota((TILES, ACOLS), 0)).astype(F32).astype(BF16)
    ns[:, 0:16] = lax.dot_general(
        jnp.concatenate([every, every], axis=1),
        pieces(wide, 1),
        (((1,), (1,)), ((), ())),
        preferred_element_type=F32,
    )
    nr[pl.ds(t, 1), :] = ns[pl.ds(t, 1), :]
    each_tile(far_first, to_owner(1, ns, nr))

    adj1[...] = adj1[...] + edges(flux_above, flux_below)
    for copy in leak_copies + bulk_copies:
        copy.wait()

    def outer(n):
        return (
            jnp.where(has_above, hr[1, n : n + 1, :], 0.0),
            jnp.where(has_below, hr[0, n : n + 1, :], 0.0),
        )

    first, last = fluxes[0:1, :], fluxes[ROWS - 1 : ROWS, :]
    factor_above, factor_below = outer(0)
    scaled_above, scaled_below = outer(1)
    diff_above, diff_below = outer(2)
    next_above = scaled_above + diff_above * first
    next_below = scaled_below + diff_below * last
    other_edges = compress(
        pad_rows(jnp.concatenate([factor_above * first, factor_below * last], axis=0), 8), block_w
    )
    leak_above = jnp.where(has_above, lr[1], 0.0) + other_edges[0:1]
    leak_below = jnp.where(has_below, lr[0], 0.0) + other_edges[1:2]
    adj_zero = (
        adj1[...] + laplace_inner(diff[...] * adj1[...]) + edges(next_above, next_below)
    )
    lap_mid = laplace_inner(mid_v[...].astype(F32)) + edges(*outer(4))
    lap_start = laplace_inner(startv[...]) + edges(*outer(3))
    local_g = block_sums(
        factor[...] * (seed_v[...].astype(F32) * lap_mid + adj1[...] * lap_start), block_w
    )

    all_of(0, ms, mr).wait()
    turned = mr[...].T[0:64]
    spread = (iota((TILES, ACOLS), 1) // 4 == iota((TILES, ACOLS), 0)).astype(F32).astype(BF16)
    copied = jnp.dot(pieces(turned, 0), spread, preferred_element_type=F32)
    copied = copied[0:64] + copied[64:128]
    col = iota((16, ACOLS), 1) % 4
    coarse = jnp.zeros((16, ACOLS), F32)
    for c in range(4):
        coarse = jnp.where(col == c, copied[16 * c : 16 * c + 16], coarse)
    w_zero = coarse[0:4] + coarse[4:8] * jnp.concatenate([leak_above, leak_own, leak_below], axis=0)
    mid_w = w_zero[1:3]
    around = lanes_by(mid_w, 1) + lanes_by(mid_w, -1) + w_zero[0:2] + w_zero[2:4] + coarse[13:15]
    recharge = mid_w + coarse[9:11] * around
    source = prolong(recharge) - adj_zero
    infil_again = prolong(infil_v[...]) * factor[...]
    depth_o[...] = (adj_zero + infil_again * source).astype(BF16)
    local_w = block_sums(factor[...] * depth_v[...].astype(F32) * source, block_w)

    def event_copies(n, buf):
        return [
            pltpu.make_async_remote_copy(
                src_ref=buf.at[e],
                dst_ref=buf.at[e],
                send_sem=ev_send.at[n, k],
                recv_sem=ev_recv.at[n, k],
                device_id=((e + k) % EVENTS, t),
                device_id_type=MESH,
            )
            for k in range(1, EVENTS)
        ]

    ev1[e] = jnp.concatenate([local_w, local_g], axis=0)
    grad_copies = event_copies(0, ev1)
    for copy in grad_copies:
        copy.start()

    for copy in head_copies:
        copy.wait()
    slot = iota((8, AROWS), 0)
    column = OWN * t + slot - jnp.where(slot < 6, 0, 8)
    known = jnp.where((column >= 0) & (column < ACOLS), 1.0, 0.0)
    c_all = cw[0:LAYERS] * known[None]
    w_all = cw[LAYERS : 2 * LAYERS] * known[None]
    lk_all = cw[2 * LAYERS] * known
    blank = jnp.zeros((1, 8, AROWS), F32)

    def layered(field):
        return jnp.concatenate([field[1:], blank], axis=0) + jnp.concatenate(
            [blank, field[:-1]], axis=0
        )

    w_next = c_all * (neighbours4(w_all) + layered(w_all))
    base = (neighbours4(w_next) + layered(w_next))[:, 0:OWN, :]
    head_o[3:LAYERS] = base[3:LAYERS]

    all_of(1, ns, nr).wait()
    xs[...] = nr[...].T
    both = jnp.concatenate([xs[pl.ds(0, 8, stride=2), :], xs[pl.ds(1, 8, stride=2), :]], axis=1)
    half, spot = iota((256, AROWS), 0), iota((256, AROWS), 1)
    place = (spot == 2 * (half % TILES) + half // TILES).astype(F32).astype(BF16)
    leak = jnp.dot(pieces(both, 0), place, preferred_element_type=F32)
    leak = leak[0:8] + leak[8:16]
    ev2[e] = top_v[...] * leak[0:OWN]
    lk_copies = event_copies(1, ev2)
    for copy in lk_copies:
        copy.start()
    more_w = lk_all * leak
    next_zero = c_all[0] * neighbours4(more_w)
    next_one = c_all[1] * more_w
    charge_o[...] = (w_all[0] + w_next[0] + more_w + next_zero)[0:OWN]
    head_o[0] = base[0] + (neighbours4(next_zero) + next_one)[0:OWN]
    head_o[1] = base[1] + (next_zero + neighbours4(next_one))[0:OWN]
    head_o[2] = base[2] + next_one[0:OWN]

    for copy in grad_copies:
        copy.wait()
    total = ev1[0] + ev1[1] + ev1[2] + ev1[3]
    gw_o[...] = total[0:2]
    gg_o[...] = total[2:4]
    for copy in lk_copies:
        copy.wait()
    glk_o[...] = ev2[0] + ev2[1] + ev2[2] + ev2[3]


def hand_over(*refs):
    half = len(refs) // 2
    for source, target in zip(refs[:half], refs[half:]):
        target[...] = source[...]


def per_device(
    surf_depth, surf_mid, surf_seed, stream, infil, diffus, leakance, active, jacobi_coef, head_seed, top_head
):
    args = (
        surf_seed[0], stream, diffus, jacobi_coef, active, leakance, head_seed[0], infil,
        surf_depth[0], surf_mid[0], top_head[0],
    )
    outs = [
        jax.ShapeDtypeStruct(shape, dtype)
        for shape, dtype in (
            ((ROWS, COLS), BF16),
            ((LAYERS, OWN, AROWS), F32),
            ((OWN, AROWS), F32),
            ((2, ACOLS), F32),
            ((2, ACOLS), F32),
            ((OWN, AROWS), F32),
        )
    ]
    vmem = pl.BlockSpec(memory_space=pltpu.VMEM)
    hbm = pl.BlockSpec(memory_space=pltpu.HBM)
    field = pltpu.VMEM((ROWS, COLS), F32)
    results = pl.pallas_call(
        step_kernel,
        out_shape=outs,
        in_specs=[hbm] * len(args),
        out_specs=[vmem] * len(outs),
        scratch_shapes=[pltpu.VMEM(a.shape, a.dtype) for a in args]
        + [field] * 6
        + [
            pltpu.VMEM((1024, 128), BF16),
            pltpu.VMEM((2, 1, COLS), F32),
            pltpu.VMEM((2, 1, COLS), F32),
            pltpu.VMEM((2, 5, COLS), F32),
            pltpu.VMEM((2, 5, COLS), F32),
            pltpu.VMEM((2, 1, ACOLS), F32),
            pltpu.VMEM((2, 1, ACOLS), F32),
            pltpu.VMEM((2 * LAYERS + 1, 8, AROWS), F32),
            pltpu.VMEM((128, 128), F32),
            pltpu.VMEM((TILES, 128), F32),
            pltpu.VMEM((TILES, 128), F32),
            pltpu.VMEM((TILES, 128), F32),
            pltpu.VMEM((TILES, 128), F32),
            pltpu.VMEM((EVENTS, 4, ACOLS), F32),
            pltpu.VMEM((EVENTS, OWN, AROWS), F32),
            pltpu.SemaphoreType.DMA((len(args),)),
            pltpu.SemaphoreType.DMA((8,)),
            pltpu.SemaphoreType.DMA((8,)),
            pltpu.SemaphoreType.DMA((2,)),
            pltpu.SemaphoreType.DMA((2,)),
            pltpu.SemaphoreType.DMA((2, EVENTS)),
            pltpu.SemaphoreType.DMA((2, EVENTS)),
        ],
        compiler_params=pltpu.CompilerParams(
            collective_id=0, has_side_effects=True, vmem_limit_bytes=63 * 1024 * 1024
        ),
    )(*args)
    depth, head, charge, grad_w, grad_g, grad_lk = pl.pallas_call(
        hand_over, out_shape=outs, in_specs=[vmem] * len(outs), out_specs=[vmem] * len(outs)
    )(*results)
    return depth[None], head[None], charge[None], grad_w, grad_g, grad_lk


def solution(mesh):
    return jax.shard_map(
        per_device,
        mesh=mesh,
        in_specs=(
            P("event", "tile", None),
            P("event", "tile", None),
            P("event", "tile", None),
            P("tile", None),
            P("tile", None),
            P("tile", None),
            P("tile", None),
            P("tile", None),
            P(None, "tile", None),
            P("event", None, "tile", None),
            P("event", "tile", None),
        ),
        out_specs=(
            P("event", "tile", None),
            P("event", None, "tile", None),
            P("event", "tile", None),
            P("tile", None),
            P("tile", None),
            P("tile", None),
        ),
        check_vma=False,
    )
```

time: 169 us -> 40.8 us (0.24)
  starting transfers between devices: 86.5 us -> 0 us
  Pallas kernels: 0 us -> 40 us
  local copies, waits for them, and re-layouts: 36 us -> 0 us
  blocking collectives: 18.3 us -> 0 us
  waiting for transfers between devices: 17.3 us -> 0 us
  other arithmetic: 9.66 us -> 0 us
    ppermute x12 -> x0, starting transfers between devices: 43.3 us -> none  [the longest x6 35.5 us: padded(): lax.ppermute(tail, axis, [(i, (i + 1) % count) for i in range(ends)])]
    all_to_all x2 -> x0, starting transfers between devices: 43.2 us -> none  [the longest x1 27 us: per_device(): lax.all_to_all(jnp.swapaxes(leak_sum, 1, 2), 'tile', split_axis=1, concat...]
    pallas_call x0 -> x2, Pallas kernels: none -> 40 us  [the longest x1 38.3 us: per_device(): pl.pallas_call(step_kernel, out_shape=outs, in_specs=[hbm] * len(args), o...]
    reshape x5 -> x0, local copies, waits for them, and re-layouts: 18.8 us -> none  [the longest x3 10.8 us: restrict_sum(): blocks = field.reshape(shape[:-2] + (shape[-2] // 8, 8, shape[-1] // 8, 8))]
    psum x1 -> x0, blocking collectives: 18.3 us -> none  [per_device(): grad_w, grad_g, grad_lk = lax.psum((local_w, local_g, local_lk), 'event')]
    all_to_all x2 -> x0, waiting for transfers between devices: 15.9 us -> none  [the longest x1 9.29 us: per_device(): lax.all_to_all(charge, 'tile', split_axis=2, concat_axis=1, tiled=True)]
    broadcast_in_dim x4 -> x0, local copies, waits for them, and re-layouts: 11.9 us -> none  [prolong(): jnp.broadcast_to(coarse[..., :, None, :, None], shape[:-2] + (shape[-2],...]
    reduce_sum x4 -> x0, other arithmetic: 7.64 us -> none  [the longest x3 7.62 us: restrict_sum(): return jnp.sum(blocks, axis=(-3, -1))]
  transfers between devices with their start and end apart: 14 -> 0, of which waited for: 4 -> 0; matrix products, arithmetic and copies ran while one was open for 14% -> 0% of each run, Pallas kernels for 0% -> 0%
where the time goes in v1:
time: 40.8 us; the launch traced here: 40.6 us
  Pallas kernels  40 us (98%)
  between operations  0.64 us (2%)
    pallas_call x1, Pallas kernels, per_device(): pl.pallas_call(step_kernel, out_shape=outs, in_specs=[hbm] * len(args), o...  38.3 us
    pallas_call x1, Pallas kernels, per_device(): pl.pallas_call(hand_over, out_shape=outs, in_specs=[vmem] * len(outs), ou...  1.65 us

profile of v1, /device:TPU:1, one launch (start us, length us, event | category | flops | bytes accessed | tf_op | source)
XLA Modules:
  0.0 40.6 jit_solution(51113138205393671)
XLA Ops:
  0.6 38.3 %shard_map.154 = (bf16[16,4096]{1,0:T(8,128)(2,1)}, f32[16,4,256]{2,1,0:T(4,128)}, f32[4,256]{1,0:T(4,128)}, f32[2,512]{1,0:T(2,128)}, f32[2,512]{1,0:T(2,128)}, /*index=5*/f32[4,256]{1,0:T(4,128)}) custom-call(bf16[16,4096]{1,0:T(8,128)(2,1)} %bitcast.8, s32[16,4096]{1,0:T(8,128)} %stream_h.1, f32[2,512]{1,0:T(2,128)} %diffus_h.1, f32[16,4,256]{2,1,0:T(4,128)} %jac_h.1, ...), custom_call_target="tpu_custom_call" | custom-call | tf_op jit(solution)/shard_map/pallas_call | solution.py:407
  39.0 1.6 %shard_map.155 = (bf16[16,4096]{1,0:T(8,128)(2,1)}, f32[16,4,256]{2,1,0:T(4,128)}, f32[4,256]{1,0:T(4,128)}, f32[2,512]{1,0:T(2,128)}, f32[2,512]{1,0:T(2,128)}, /*index=5*/f32[4,256]{1,0:T(4,128)}) custom-call(bf16[16,4096]{1,0:T(8,128)(2,1)} %get-tuple-element.18.refs_0_, f32[16,4,256]{2,1,0:T(4,128)} %get-tuple-element.19.refs_1_, ...), custom_call_target="tpu_custom_call" | custom-call | tf_op jit(solution)/shard_map/pallas_call | solution.py:442

commit v2 on v1

--- a/solution.py
+++ b/solution.py
@@ -76,6 +76,22 @@
     return jnp.concatenate(halves, axis=0)
 
 
+def prolong_rows(coarse):
+    spot = iota((8, 128), 1) // 8
+    return jnp.concatenate(
+        [
+            jnp.take_along_axis(
+                coarse[:, (m // 8) * 128 : (m // 8 + 1) * 128],
+                spot + 16 * (m % 8),
+                axis=1,
+                mode="promise_in_bounds",
+            )
+            for m in range(COLS // 128)
+        ],
+        axis=1,
+    )
+
+
 def pad_rows(rows, n):
     return jnp.concatenate([rows, jnp.zeros((n - rows.shape[0], rows.shape[1]), F32)], axis=0)
 
@@ -94,8 +110,8 @@
     seed_h, stream_h, diffus_h, jac_h, act_h, leak_h, head_h, infil_h, depth_h, mid_h, top_h,
     depth_o, head_o, charge_o, gw_o, gg_o, glk_o,
     seed_v, stream_v, diffus_v, jac_v, act_v, leak_v, head_v, infil_v, depth_v, mid_v, top_v,
-    factor, diff, fluxes, adj1, scaled, startv, block_w,
-    fs, fr, hs, hr, ls, lr, cw, xs, ms, mr, ns, nr, ev1, ev2,
+    factor, diff, fluxes, adj1, scaled, startv, infilf, block_w,
+    fs, fr, hs, hr, gs, gr, ls, lr, cw, xs, ms, mr, ns, nr, ev1, ev2,
     in_sem, edge_send, edge_recv, a2a_send, a2a_recv, ev_send, ev_recv,
 ):
     e = lax.axis_index("event")
@@ -155,17 +171,17 @@
     adj1[...] = seed + laplace_inner(fluxes[...])
     leak_part = block_sums(factor[...] * (adj1[...] + seed), block_w)
     scaled[...] = diff[...] * adj1[...]
-    infil_fine = prolong(infil_v[...]) * factor[...]
+    infilf[...] = prolong(infil_v[...]) * factor[...]
     depth = depth_v[...].astype(F32)
-    startv[...] = depth - infil_fine * depth
+    startv[...] = depth - infilf[...] * depth
     middle = mid_v[...].astype(F32)
     for way, at in ((0, 0), (1, ROWS - 1)):
         hs[way, 0:1, :] = factor[at : at + 1, :]
         hs[way, 1:2, :] = scaled[at : at + 1, :]
-        hs[way, 2:3, :] = diff[at : at + 1, :]
-        hs[way, 3:4, :] = startv[at : at + 1, :]
-        hs[way, 4:5, :] = middle[at : at + 1, :]
-        ls[way] = leak_part[way : way + 1]
+        gs[way, 0:1, :] = startv[at : at + 1, :]
+        gs[way, 1:2, :] = middle[at : at + 1, :]
+        ls[way, 0:1, :] = leak_part[way : way + 1]
+        ls[way, 1:2, :] = diffus_v[way : way + 1, :]
 
     coeffs = act_v[...].astype(F32)[None] * jac_v[...]
     weighted = coeffs * head_v[...]
@@ -199,13 +215,25 @@
         )
 
     flux_copies = [edge_copy(0, fs.at[0], fr.at[0], above), edge_copy(1, fs.at[1], fr.at[1], below)]
-    leak_copies = [edge_copy(2, ls.at[0], lr.at[0], above), edge_copy(3, ls.at[1], lr.at[1], below)]
-    bulk_copies = [edge_copy(4, hs.at[0], hr.at[0], above), edge_copy(5, hs.at[1], hr.at[1], below)]
+    bulk_copies = [
+        edge_copy(2, ls.at[0], lr.at[0], above),
+        edge_copy(3, ls.at[1], lr.at[1], below),
+        edge_copy(4, hs.at[0], hr.at[0], above),
+        edge_copy(5, hs.at[1], hr.at[1], below),
+    ]
+    late_copies = [edge_copy(6, gs.at[0], gr.at[0], above), edge_copy(7, gs.at[1], gr.at[1], below)]
+    heads = pl.ds(LAYERS, LAYERS + 1)
     head_copies = [
-        edge_copy(6, cw.at[:, pl.ds(0, 2), :], cw.at[:, pl.ds(4, 2), :], above),
-        edge_copy(7, cw.at[:, pl.ds(2, 2), :], cw.at[:, pl.ds(6, 2), :], below),
+        edge_copy(8, cw.at[heads, pl.ds(0, 2), :], cw.at[heads, pl.ds(4, 2), :], above),
+        edge_copy(9, cw.at[heads, pl.ds(2, 2), :], cw.at[heads, pl.ds(6, 2), :], below),
+        edge_copy(
+            10, cw.at[pl.ds(0, LAYERS), pl.ds(0, 1), :], cw.at[pl.ds(0, LAYERS), pl.ds(4, 1), :], above
+        ),
+        edge_copy(
+            11, cw.at[pl.ds(0, LAYERS), pl.ds(3, 1), :], cw.at[pl.ds(0, LAYERS), pl.ds(7, 1), :], below
+        ),
     ]
-    for copy in flux_copies + leak_copies + bulk_copies:
+    for copy in flux_copies + bulk_copies:
         copy.start()
 
     def to_owner(n, src, dst):
@@ -233,8 +261,20 @@
 
     mr[pl.ds(t, 1), :] = ms[pl.ds(t, 1), :]
     each_tile(far_first, to_owner(0, ms, mr))
-    for copy in head_copies:
+    for copy in late_copies + head_copies:
         copy.start()
+
+    start_inner = laplace_inner(startv[...])
+    start_ends = (start_inner[0:1], start_inner[ROWS - 1 : ROWS])
+    part_g = block_sums(
+        factor[...]
+        * (
+            seed_v[...].astype(F32) * laplace_inner(mid_v[...].astype(F32))
+            + adj1[...] * start_inner
+        ),
+        block_w,
+    )
+    water = block_sums(factor[...] * depth_v[...].astype(F32), block_w)
 
     for copy in flux_copies:
         copy.wait()
@@ -264,34 +304,31 @@
     each_tile(far_first, to_owner(1, ns, nr))
 
     adj1[...] = adj1[...] + edges(flux_above, flux_below)
-    for copy in leak_copies + bulk_copies:
-        copy.wait()
-
-    def outer(n):
+    for copy in bulk_copies:
+        copy.wait()
+
+    def outer(ref, n):
         return (
-            jnp.where(has_above, hr[1, n : n + 1, :], 0.0),
-            jnp.where(has_below, hr[0, n : n + 1, :], 0.0),
+            jnp.where(has_above, ref[1, n : n + 1, :], 0.0),
+            jnp.where(has_below, ref[0, n : n + 1, :], 0.0),
         )
 
     first, last = fluxes[0:1, :], fluxes[ROWS - 1 : ROWS, :]
-    factor_above, factor_below = outer(0)
-    scaled_above, scaled_below = outer(1)
-    diff_above, diff_below = outer(2)
-    next_above = scaled_above + diff_above * first
-    next_below = scaled_below + diff_below * last
+    factor_above, factor_below = outer(hr, 0)
+    scaled_above, scaled_below = outer(hr, 1)
+    spread_ends = prolong_rows(pad_rows(jnp.concatenate([lr[1, 1:2, :], lr[0, 1:2, :]], axis=0), 8))
+    next_above = scaled_above + spread_ends[0:1] * factor_above * first
+    next_below = scaled_below + spread_ends[1:2] * factor_below * last
     other_edges = compress(
         pad_rows(jnp.concatenate([factor_above * first, factor_below * last], axis=0), 8), block_w
     )
-    leak_above = jnp.where(has_above, lr[1], 0.0) + other_edges[0:1]
-    leak_below = jnp.where(has_below, lr[0], 0.0) + other_edges[1:2]
+    leak_above = jnp.where(has_above, lr[1, 0:1, :], 0.0) + other_edges[0:1]
+    leak_below = jnp.where(has_below, lr[0, 0:1, :], 0.0) + other_edges[1:2]
     adj_zero = (
         adj1[...] + laplace_inner(diff[...] * adj1[...]) + edges(next_above, next_below)
     )
-    lap_mid = laplace_inner(mid_v[...].astype(F32)) + edges(*outer(4))
-    lap_start = laplace_inner(startv[...]) + edges(*outer(3))
-    local_g = block_sums(
-        factor[...] * (seed_v[...].astype(F32) * lap_mid + adj1[...] * lap_start), block_w
-    )
+    scaled[...] = adj_zero
+    drained = block_sums(factor[...] * depth_v[...].astype(F32) * adj_zero, block_w)
 
     all_of(0, ms, mr).wait()
     turned = mr[...].T[0:64]
@@ -306,10 +343,22 @@
     mid_w = w_zero[1:3]
     around = lanes_by(mid_w, 1) + lanes_by(mid_w, -1) + w_zero[0:2] + w_zero[2:4] + coarse[13:15]
     recharge = mid_w + coarse[9:11] * around
-    source = prolong(recharge) - adj_zero
-    infil_again = prolong(infil_v[...]) * factor[...]
-    depth_o[...] = (adj_zero + infil_again * source).astype(BF16)
-    local_w = block_sums(factor[...] * depth_v[...].astype(F32) * source, block_w)
+    local_w = water * recharge - drained
+    for copy in late_copies:
+        copy.wait()
+    start_above, start_below = outer(gr, 0)
+    mid_above, mid_below = outer(gr, 1)
+    seed_edges = seed_v[...].astype(F32)
+    edge_above = factor[0:1, :] * (
+        seed_edges[0:1] * mid_above + flux_above * start_ends[0] + adj1[0:1, :] * start_above
+    )
+    edge_below = factor[ROWS - 1 : ROWS, :] * (
+        seed_edges[ROWS - 1 : ROWS] * mid_below
+        + flux_below * start_ends[1]
+        + adj1[ROWS - 1 : ROWS, :] * start_below
+    )
+    edge_g = compress(pad_rows(jnp.concatenate([edge_above, edge_below], axis=0), 8), block_w)
+    local_g = part_g + edge_g[0:2]
 
     def event_copies(n, buf):
         return [
@@ -329,12 +378,15 @@
     for copy in grad_copies:
         copy.start()
 
+    depth_o[...] = (scaled[...] + infilf[...] * (prolong(recharge) - scaled[...])).astype(BF16)
+
     for copy in head_copies:
         copy.wait()
     slot = iota((8, AROWS), 0)
     column = OWN * t + slot - jnp.where(slot < 6, 0, 8)
     known = jnp.where((column >= 0) & (column < ACOLS), 1.0, 0.0)
-    c_all = cw[0:LAYERS] * known[None]
+    offset = iota((LAYERS, 8, AROWS), 1)
+    c_all = jnp.where((offset == 5) | (offset == 6), 0.0, cw[0:LAYERS]) * known[None]
     w_all = cw[LAYERS : 2 * LAYERS] * known[None]
     lk_all = cw[2 * LAYERS] * known
     blank = jnp.zeros((1, 8, AROWS), F32)
@@ -378,9 +430,16 @@
 
 
 def hand_over(*refs):
+    sem = refs[-1]
     half = len(refs) // 2
-    for source, target in zip(refs[:half], refs[half:]):
-        target[...] = source[...]
+    copies = [
+        pltpu.make_async_copy(source, target, sem.at[n])
+        for n, (source, target) in enumerate(zip(refs[:half], refs[half:-1]))
+    ]
+    for copy in copies:
+        copy.start()
+    for copy in copies:
+        copy.wait()
 
 
 def per_device(
@@ -410,15 +469,17 @@
         in_specs=[hbm] * len(args),
         out_specs=[vmem] * len(outs),
         scratch_shapes=[pltpu.VMEM(a.shape, a.dtype) for a in args]
-        + [field] * 6
+        + [field] * 7
         + [
             pltpu.VMEM((1024, 128), BF16),
             pltpu.VMEM((2, 1, COLS), F32),
             pltpu.VMEM((2, 1, COLS), F32),
-            pltpu.VMEM((2, 5, COLS), F32),
-            pltpu.VMEM((2, 5, COLS), F32),
-            pltpu.VMEM((2, 1, ACOLS), F32),
-            pltpu.VMEM((2, 1, ACOLS), F32),
+            pltpu.VMEM((2, 2, COLS), F32),
+            pltpu.VMEM((2, 2, COLS), F32),
+            pltpu.VMEM((2, 2, COLS), F32),
+            pltpu.VMEM((2, 2, COLS), F32),
+            pltpu.VMEM((2, 2, ACOLS), F32),
+            pltpu.VMEM((2, 2, ACOLS), F32),
             pltpu.VMEM((2 * LAYERS + 1, 8, AROWS), F32),
             pltpu.VMEM((128, 128), F32),
             pltpu.VMEM((TILES, 128), F32),
@@ -428,19 +489,24 @@
             pltpu.VMEM((EVENTS, 4, ACOLS), F32),
             pltpu.VMEM((EVENTS, OWN, AROWS), F32),
             pltpu.SemaphoreType.DMA((len(args),)),
-            pltpu.SemaphoreType.DMA((8,)),
-            pltpu.SemaphoreType.DMA((8,)),
+            pltpu.SemaphoreType.DMA((12,)),
+            pltpu.SemaphoreType.DMA((12,)),
             pltpu.SemaphoreType.DMA((2,)),
             pltpu.SemaphoreType.DMA((2,)),
             pltpu.SemaphoreType.DMA((2, EVENTS)),
             pltpu.SemaphoreType.DMA((2, EVENTS)),
         ],
         compiler_params=pltpu.CompilerParams(
-            collective_id=0, has_side_effects=True, vmem_limit_bytes=63 * 1024 * 1024
-        ),
-    )(*args)
+            collective_id=0, has_side_effects=True, vmem_limit_bytes=40 * 1024 * 1024
+        ),
+    )(*[pltpu.with_memory_space_constraint(a, pltpu.HBM) for a in args])
     depth, head, charge, grad_w, grad_g, grad_lk = pl.pallas_call(
-        hand_over, out_shape=outs, in_specs=[vmem] * len(outs), out_specs=[vmem] * len(outs)
+        hand_over,
+        out_shape=outs,
+        in_specs=[pl.BlockSpec(memory_space=pl.ANY)] * len(outs),
+        out_specs=[hbm] * len(outs),
+        scratch_shapes=[pltpu.SemaphoreType.DMA((len(outs),))],
+        compiler_params=pltpu.CompilerParams(vmem_limit_bytes=1024 * 1024),
     )(*results)
     return depth[None], head[None], charge[None], grad_w, grad_g, grad_lk
 

time: 40.8 us -> 38.3 us (0.939)
  Pallas kernels: 40 us -> 37.5 us
    pallas_call x1, Pallas kernels: 38.3 us -> 36.8 us  [per_device(): pl.pallas_call(step_kernel, out_shape=outs, in_specs=[hbm] * len(args), o...]
    pallas_call x1, Pallas kernels: 1.65 us -> 0.74 us  [per_device(): pl.pallas_call(hand_over, out_shape=outs, in_specs=[pl.BlockSpec(memory_s...]
where the time goes in v2:
time: 38.3 us; the launch traced here: 38.2 us
  Pallas kernels  37.5 us (98%)
  between operations  0.64 us (2%)
    pallas_call x1, Pallas kernels, per_device(): pl.pallas_call(step_kernel, out_shape=outs, in_specs=[hbm] * len(args), o...  36.8 us

profile of v2, /device:TPU:1, one launch (start us, length us, event | category | flops | bytes accessed | tf_op | source)
XLA Modules:
  0.0 38.2 jit_solution(806706888108060204)
XLA Ops:
  0.6 36.8 %shard_map.154 = (bf16[16,4096]{1,0:T(8,128)(2,1)S(1)}, f32[16,4,256]{2,1,0:T(4,128)S(1)}, f32[4,256]{1,0:T(4,128)S(1)}, f32[2,512]{1,0:T(2,128)S(1)}, f32[2,512]{1,0:T(2,128)S(1)}, /*index=5*/f32[4,256]{1,0:T(4,128)S(1)}) custom-call(bf16[16,4096]{1,0:T(8,128)(2,1)} %bitcast.8, s32[16,4096]{1,0:T(8,128)} %stream_h.1, f32[2,512]{1,0:T(2,128)} %diffus_h.1, ...), custom_call_target="tpu_custom_call" | custom-call | tf_op jit(solution)/shard_map/pallas_call | solution.py:466
  37.4 0.7 %shard_map.155 = (bf16[16,4096]{1,0:T(8,128)(2,1)}, f32[16,4,256]{2,1,0:T(4,128)}, f32[4,256]{1,0:T(4,128)}, f32[2,512]{1,0:T(2,128)}, f32[2,512]{1,0:T(2,128)}, /*index=5*/f32[4,256]{1,0:T(4,128)}) custom-call(bf16[16,4096]{1,0:T(8,128)(2,1)S(1)} %get-tuple-element.18.refs_0_, f32[16,4,256]{2,1,0:T(4,128)S(1)} %get-tuple-element.19.refs_1_, ...), custom_call_target="tpu_custom_call" | custom-call | tf_op jit(solution)/shard_map/pallas_call | solution.py:503

commit v3 on v2

--- a/solution.py
+++ b/solution.py
@@ -111,7 +111,7 @@
     depth_o, head_o, charge_o, gw_o, gg_o, glk_o,
     seed_v, stream_v, diffus_v, jac_v, act_v, leak_v, head_v, infil_v, depth_v, mid_v, top_v,
     factor, diff, fluxes, adj1, scaled, startv, infilf, block_w,
-    fs, fr, hs, hr, gs, gr, ls, lr, cw, xs, ms, mr, ns, nr, ev1, ev2,
+    fs, fr, hs, hr, gs, gr, ls, lr, cw, xs, ms, mr, ns, nr, ev1, ev2, every_w, place_w,
     in_sem, edge_send, edge_recv, a2a_send, a2a_recv, ev_send, ev_recv,
 ):
     e = lax.axis_index("event")
@@ -149,6 +149,8 @@
         load.start()
 
     barrier = pltpu.get_barrier_semaphore()
+    for near in (above, below):
+        pl.semaphore_signal(barrier, inc=1, device_id=(e, near), device_id_type=MESH)
     for k in range(1, EVENTS):
         pl.semaphore_signal(barrier, inc=1, device_id=((e + k) % EVENTS, t), device_id_type=MESH)
     each_tile(
@@ -202,7 +204,7 @@
         preferred_element_type=F32,
     )
 
-    pl.semaphore_wait(barrier, TILES - 1 + EVENTS - 1)
+    pl.semaphore_wait(barrier, TILES - 1 + EVENTS - 1 + 2)
 
     def edge_copy(n, src, dst, target):
         return pltpu.make_async_remote_copy(
@@ -264,6 +266,12 @@
     for copy in late_copies + head_copies:
         copy.start()
 
+    every = (iota((TILES, ACOLS), 1) == 4 * iota((TILES, ACOLS), 0)).astype(F32).astype(BF16)
+    every_w[...] = jnp.concatenate([every, every], axis=1)
+    half, spot = iota((256, AROWS), 0), iota((256, AROWS), 1)
+    place = (spot == 2 * (half % TILES) + half // TILES).astype(F32).astype(BF16)
+    place_w[...] = place
+
     start_inner = laplace_inner(startv[...])
     start_ends = (start_inner[0:1], start_inner[ROWS - 1 : ROWS])
     part_g = block_sums(
@@ -293,9 +301,8 @@
     wide = jnp.concatenate(
         [lanes_by(leak_own, -c) if c else leak_own for c in (0, 1, 2, 3, 4, 5, -2, -1)], axis=0
     )
-    every = (iota((TILES, ACOLS), 1) == 4 * iota((TILES, ACOLS), 0)).astype(F32).astype(BF16)
     ns[:, 0:16] = lax.dot_general(
-        jnp.concatenate([every, every], axis=1),
+        every_w[...],
         pieces(wide, 1),
         (((1,), (1,)), ((), ())),
         preferred_element_type=F32,
@@ -403,9 +410,7 @@
     all_of(1, ns, nr).wait()
     xs[...] = nr[...].T
     both = jnp.concatenate([xs[pl.ds(0, 8, stride=2), :], xs[pl.ds(1, 8, stride=2), :]], axis=1)
-    half, spot = iota((256, AROWS), 0), iota((256, AROWS), 1)
-    place = (spot == 2 * (half % TILES) + half // TILES).astype(F32).astype(BF16)
-    leak = jnp.dot(pieces(both, 0), place, preferred_element_type=F32)
+    leak = jnp.dot(pieces(both, 0), place_w[...], preferred_element_type=F32)
     leak = leak[0:8] + leak[8:16]
     ev2[e] = top_v[...] * leak[0:OWN]
     lk_copies = event_copies(1, ev2)
@@ -488,6 +493,8 @@
             pltpu.VMEM((TILES, 128), F32),
             pltpu.VMEM((EVENTS, 4, ACOLS), F32),
             pltpu.VMEM((EVENTS, OWN, AROWS), F32),
+            pltpu.VMEM((TILES, 2 * ACOLS), BF16),
+            pltpu.VMEM((256, AROWS), BF16),
             pltpu.SemaphoreType.DMA((len(args),)),
             pltpu.SemaphoreType.DMA((12,)),
             pltpu.SemaphoreType.DMA((12,)),

time: 38.3 us -> 38.3 us (level)
  no operation moved by 1% of the time
where the time goes in v3:
time: 38.3 us; the launch traced here: 38.2 us
  Pallas kernels  37.5 us (98%)
  between operations  0.64 us (2%)
    pallas_call x1, Pallas kernels, per_device(): pl.pallas_call(step_kernel, out_shape=outs, in_specs=[hbm] * len(args), o...  36.8 us

profile of v3, /device:TPU:1, one launch (start us, length us, event | category | flops | bytes accessed | tf_op | source)
XLA Modules:
  0.0 38.2 jit_solution(11333524639084132082)
XLA Ops:
  0.6 36.8 %shard_map.154 = (bf16[16,4096]{1,0:T(8,128)(2,1)S(1)}, f32[16,4,256]{2,1,0:T(4,128)S(1)}, f32[4,256]{1,0:T(4,128)S(1)}, f32[2,512]{1,0:T(2,128)S(1)}, f32[2,512]{1,0:T(2,128)S(1)}, /*index=5*/f32[4,256]{1,0:T(4,128)S(1)}) custom-call(bf16[16,4096]{1,0:T(8,128)(2,1)} %bitcast.8, s32[16,4096]{1,0:T(8,128)} %stream_h.1, f32[2,512]{1,0:T(2,128)} %diffus_h.1, ...), custom_call_target="tpu_custom_call" | custom-call | tf_op jit(solution)/shard_map/pallas_call | solution.py:471
  37.4 0.7 %shard_map.155 = (bf16[16,4096]{1,0:T(8,128)(2,1)}, f32[16,4,256]{2,1,0:T(4,128)}, f32[4,256]{1,0:T(4,128)}, f32[2,512]{1,0:T(2,128)}, f32[2,512]{1,0:T(2,128)}, /*index=5*/f32[4,256]{1,0:T(4,128)}) custom-call(bf16[16,4096]{1,0:T(8,128)(2,1)S(1)} %get-tuple-element.18.refs_0_, f32[16,4,256]{2,1,0:T(4,128)S(1)} %get-tuple-element.19.refs_1_, ...), custom_call_target="tpu_custom_call" | custom-call | tf_op jit(solution)/shard_map/pallas_call | solution.py:510
